TPU v7x, 512 devices: a whole 4x4x16 slice. The times are simulated.
512 devices in a mesh: leaf: 64 (over y, z), dom: 2 (over core), rep: 4 (over x).
Axes of the slice: x: 4, y: 4, z: 16, core: 2. Of those that a mesh axis runs over, the one named last changes fastest.
Arguments:
- leaf_basis: bfloat16 [2048, 512, 128], P(('leaf', 'dom', 'rep')), as said below
- transfer: float32 [3584, 128, 128], P(('leaf', 'dom', 'rep')), as said below
- transfer_top: float32 [256, 128, 128], P(('leaf', 'dom')), as said below
- coupling_parts: bfloat16 [4, 8192, 128, 128], P('rep', ('leaf', 'dom')), may hold values from -1 to 1
- row_slot: int32 [8192], P(('leaf', 'dom', 'rep')), may hold values from 0 to 6, as said below
- col_node: int32 [8192], P(('leaf', 'dom', 'rep')), may hold values from 0 to 3583, as said below
Outputs:
- leaf_orth: bfloat16 [2048, 512, 128], P(('leaf', 'dom', 'rep'))
- new_transfer: float32 [3584, 128, 128], P(('leaf', 'dom', 'rep'))
- new_top: float32 [256, 128, 128], P(('leaf', 'dom'), 'rep')
- top_factor: float32 [128, 128, 128], P(('leaf', 'dom'), 'rep')
- coupling_new: bfloat16 [8192, 128, 128], P(('leaf', 'dom', 'rep'))
Inputs may be any that keep to these rules, and one draw needn't show every extreme that they name: `leaf_basis`: every leaf block has full column rank. Every transfer factor is invertible. `transfer_top`: every transfer factor is invertible. `row_slot`: slots 0 to 3 are the holding device's four leaves, 4 and 5 its two level-1 nodes, 6 its level-2 node; the holder of block k is device position k // 16 along leaf+dom+rep. col_node[k] = 7 d + c, where d is a device position along leaf+dom+rep at most 2 away from the holder of block k and c is a slot of the same level as row_slot[k] (0 to 3, 4 to 5, or 6); the first block of every device has its column node exactly 2 positions away.
All inputs are finite; a program needn't handle non-finite values.
Results may differ from a plain program's by a relative error of at most 0.013.
Values may be sent and summed in bfloat16 or wider, within the bound.
A program may use at most 64 MiB of HBM per device.

v0:
```python
import functools

import jax
import jax.numpy as jnp
from jax import lax
from jax.experimental import pallas as pl
from jax.experimental.pallas import tpu as pltpu
from jax.sharding import PartitionSpec as P

PTS = 512
N = 128
F32, BF16 = jnp.float32, jnp.bfloat16
MESH = pl.DeviceIdType.MESH
HALO = (1, -1, 2, -2)


def split3(x):
    high = x.astype(BF16)
    rest = x - high.astype(F32)
    mid = rest.astype(BF16)
    low = (rest - mid.astype(F32)).astype(BF16)
    return high, mid, low


def dot_tn(a, b):
    return lax.dot_general(a, b, (((0,), (0,)), ((), ())), preferred_element_type=F32)


def dot_nt(a, b):
    return lax.dot_general(a, b, (((1,), (1,)), ((), ())), preferred_element_type=F32)


def precise_tn(a, b):
    ah, am, al = split3(a)
    bh, bm, bl = split3(b)
    return dot_tn(
        jnp.concatenate([ah, ah, am, am, ah, al], 0),
        jnp.concatenate([bh, bm, bh, bm, bl, bh], 0),
    )


def precise_nn(a, b):
    return jnp.dot(a, b, precision=lax.Precision.HIGHEST, preferred_element_type=F32)


def precise_nt(a, b):
    return lax.dot_general(
        a, b, (((1,), (1,)), ((), ())), precision=lax.Precision.HIGHEST, preferred_element_type=F32
    )


def factor(m_ref, count, hooks=None):
    lane = lax.broadcasted_iota(jnp.int32, (1, 8, N), 2)
    sub = lax.broadcasted_iota(jnp.int32, (1, 8, N), 1)
    for j in range(N // 8):
        first = 8 * j
        rows = m_ref[:, first : first + 8, :]
        cols = [
            jnp.broadcast_to(rows[:, :, first + q : first + q + 1], (count, 8, N)) for q in range(8)
        ]
        inv = jnp.zeros((count, 8, N), F32)
        for q in range(8):
            r = 1.0 / cols[q][:, q : q + 1, :]
            inv = jnp.where(sub == q, r, inv)
            mult = jnp.where(sub > q, cols[q] * r, 0.0)
            for t in range(q + 1, 8):
                cols[t] = cols[t] - mult * cols[t][:, q : q + 1, :]
            rows = jnp.where(
                (lane == first + q) & (sub > q), -mult, rows - mult * rows[:, q : q + 1, :]
            )
        scale = jnp.sqrt(inv)
        done = rows * scale
        m_ref[:, first : first + 8, :] = done
        start = first + 8
        if start < N:
            row = first + sub
            ext = jnp.where(
                lane == row, scale, jnp.where((lane > row) & (lane < start), 0.0, done)
            )
            lanes = lax.broadcasted_iota(jnp.int32, (N - start, N), 1)
            drop = (lanes >= first) & (lanes < start)
            for m in range(count):
                update = precise_tn(done[m], ext[m])[start:]
                m_ref[m, start:, :] = jnp.where(drop, 0.0, m_ref[m, start:, :]) - update
        if hooks and j in hooks:
            hooks[j]()


def upper(x):
    r = lax.broadcasted_iota(jnp.int32, (N, N), 0)
    c = lax.broadcasted_iota(jnp.int32, (N, N), 1)
    return jnp.where(c >= r, x, 0.0)


def lower_inverse(x):
    r = lax.broadcasted_iota(jnp.int32, (N, N), 0)
    c = lax.broadcasted_iota(jnp.int32, (N, N), 1)
    return jnp.where(c < r, x, jnp.where(c == r, 1.0 / x, 0.0))


def main_kernel(
    n_leaf,
    leaf_hbm, trans_hbm, top_hbm, parts_hbm,
    orth_hbm, new_hbm, ntop_hbm, ftop_hbm, pool_hbm, sum_hbm,
    leaf_v, trans_v, top_v, mats, tops, c2, a_in, f_in, own, fwd, r_stack,
    orth_v, new_v, ntop_v, ftop_v, sum_v,
    in_sem, rs_send, rs_recv, g_send, g_recv, h_send, h_recv, out_sem,
):
    leaf, dom, rep = lax.axis_index("leaf"), lax.axis_index("dom"), lax.axis_index("rep")
    lin = (leaf * 2 + dom) * 4 + rep
    total = n_leaf * 8

    def linear(shift):
        t = lax.rem(lin + shift + total, total)
        return (lax.div(t, 8), lax.rem(lax.div(t, 4), 2), lax.rem(t, 4))

    def ring(shift):
        return lax.rem(rep + shift, 4)

    def ring_id(shift):
        return (leaf, dom, ring(shift))

    def load(src, dst, k):
        copy = pltpu.make_async_copy(src, dst, in_sem.at[k])
        copy.start()
        return copy

    load_leaf = load(leaf_hbm, leaf_v, 0)
    load_trans = load(trans_hbm, trans_v, 1)
    load_top = load(top_hbm, top_v, 2)
    load_own = load(parts_hbm.at[0, pl.ds(16 * rep, 16)], own, 3)
    load_fr = load(parts_hbm.at[0, pl.ds(16 * ring(1), 8)], fwd.at[0], 4)
    load_fl = load(parts_hbm.at[0, pl.ds(16 * ring(3) + 8, 8)], fwd.at[1], 5)

    barrier = pltpu.get_barrier_semaphore()
    for shift in (1, 2, 3):
        pl.semaphore_signal(barrier, inc=1, device_id=ring_id(shift), device_id_type=MESH)
    for shift in HALO:
        pl.semaphore_signal(barrier, inc=1, device_id=linear(shift), device_id_type=MESH)
    pl.semaphore_wait(barrier, 7)

    def remote(src, dst, send, recv, target):
        copy = pltpu.make_async_remote_copy(
            src_ref=src, dst_ref=dst, send_sem=send, recv_sem=recv,
            device_id=target, device_id_type=MESH,
        )
        copy.start()
        return copy

    def block(dest, half):
        return parts_hbm.at[0, pl.ds(16 * ring(dest) + 8 * half, 8)]

    ar = remote(block(2, 0), a_in.at[0], rs_send.at[0], rs_recv.at[0], ring_id(1))
    al = remote(block(2, 1), a_in.at[1], rs_send.at[1], rs_recv.at[1], ring_id(3))
    br = remote(block(1, 1), f_in.at[0, pl.ds(8, 8)], rs_send.at[2], rs_recv.at[2], ring_id(1))
    bl = remote(block(3, 0), f_in.at[1, pl.ds(0, 8)], rs_send.at[3], rs_recv.at[3], ring_id(3))

    load_leaf.wait()
    for i in range(4):
        u = leaf_v[i]
        mats[i] = dot_tn(u, u) * (1.0 / PTS)
    load_trans.wait()

    def lifted(g, e):
        return precise_tn(e, precise_tn(g, e))

    for p in range(2):
        mats[4 + p] = lifted(mats[2 * p], trans_v[2 * p]) + lifted(
            mats[2 * p + 1], trans_v[2 * p + 1]
        )
    mats[6] = lifted(mats[4], trans_v[4]) + lifted(mats[5], trans_v[5])
    c2[0] = lifted(mats[6], trans_v[6])
    swaps = [
        remote(c2.at[0], c2.at[s], g_send.at[s - 1], g_recv.at[s - 1], ring_id(s))
        for s in (1, 2, 3)
    ]
    second = []

    def pass_on():
        ar.wait_recv()
        load_fr.wait()
        for i in range(8):
            fwd[0, i] = (fwd[0, i].astype(F32) + a_in[0, i].astype(F32)).astype(BF16)
        second.append(
            remote(fwd.at[0], f_in.at[0, pl.ds(0, 8)], rs_send.at[4], rs_recv.at[4], ring_id(1))
        )
        al.wait_recv()
        load_fl.wait()
        for i in range(8):
            fwd[1, i] = (fwd[1, i].astype(F32) + a_in[1, i].astype(F32)).astype(BF16)
        second.append(
            remote(fwd.at[1], f_in.at[1, pl.ds(8, 8)], rs_send.at[5], rs_recv.at[5], ring_id(3))
        )

    factor(mats, 7, {10: pass_on})

    for i in range(7):
        r_stack[i] = upper(mats[i]).astype(BF16)
    halo = [
        remote(r_stack, pool_hbm.at[i], h_send.at[i], h_recv.at[i], linear(shift))
        for i, shift in enumerate(HALO)
    ]

    def store(src, dst, k):
        copy = pltpu.make_async_copy(src, dst, out_sem.at[k])
        copy.start()
        return copy

    stores = [store(r_stack, pool_hbm.at[4], 0)]

    for s in swaps:
        s.wait_recv()
    low_bit = lax.rem(rep, 2)
    high_bit = lax.div(rep, 2)
    even = low_bit == 0
    mine = c2[0] + jnp.where(even, c2[3], c2[1])
    other = c2[2] + jnp.where(even, c2[1], c2[3])
    first_node = jnp.where(high_bit == 0, mine, other)
    second_node = jnp.where(high_bit == 0, other, mine)
    load_top.wait()
    tops[0] = first_node
    tops[1] = second_node
    tops[2] = lifted(first_node, top_v[0]) + lifted(second_node, top_v[1])
    factor(tops, 3)

    for i in range(4):
        orth_v[i] = dot_nt(leaf_v[i], lower_inverse(mats[i]).astype(BF16)).astype(BF16)
    stores.append(store(orth_v, orth_hbm, 1))
    for c in range(6):
        inverse = lower_inverse(mats[4 + c // 2])
        new_v[c] = precise_nt(precise_nn(upper(mats[c]), trans_v[c]), inverse)
    own_three = jnp.where(high_bit == 0, tops[0], tops[1])
    new_v[6] = precise_nt(precise_nn(upper(mats[6]), trans_v[6]), lower_inverse(own_three))
    stores.append(store(new_v, new_hbm, 2))
    top_inverse = lower_inverse(tops[2])
    share = pl.ds(pl.multiple_of(rep * 32, 32), 32)
    row = lax.broadcasted_iota(jnp.int32, (32, N), 0) + rep * 32
    col = lax.broadcasted_iota(jnp.int32, (32, N), 1)
    keep = col >= row
    for t in range(2):
        part = jnp.where(keep, tops[t, share, :], 0.0)
        ntop_v[t] = precise_nt(precise_nn(part, top_v[t]), top_inverse)
    ftop_v[0] = jnp.where(keep, tops[2, share, :], 0.0)
    stores.append(store(ntop_v, ntop_hbm, 3))
    stores.append(store(ftop_v, ftop_hbm, 4))

    load_own.wait()
    br.wait_recv()
    bl.wait_recv()
    for s in second:
        s.wait_recv()
    for i in range(16):
        sum_v[i] = (
            own[i].astype(F32) + (f_in[0, i].astype(F32) + f_in[1, i].astype(F32))
        ).astype(BF16)
    stores.append(store(sum_v, sum_hbm, 5))
    for h in halo:
        h.wait_recv()
    for copy in [ar, al, br, bl, *swaps, *second, *halo]:
        copy.wait_send()
    for copy in stores:
        copy.wait()


def last_kernel(
    row_ref, col_ref, sum_ref, pool_ref, orth_in, new_in, ntop_in, ftop_in,
    out_ref, orth_out, new_out, ntop_out, ftop_out, sems,
):
    copies = [
        pltpu.make_async_copy(a, b, sems.at[i])
        for i, (a, b) in enumerate(
            ((orth_in, orth_out), (new_in, new_out), (ntop_in, ntop_out), (ftop_in, ftop_out))
        )
    ]
    for c in copies:
        c.start()
    me = (lax.axis_index("leaf") * 2 + lax.axis_index("dom")) * 4 + lax.axis_index("rep")
    for k in range(16):
        node = col_ref[k]
        device = lax.div(node, 7)
        slot = node - 7 * device
        shift = device - me
        place = jnp.where(shift == 0, 4, jnp.where(shift == -1, 0, jnp.where(shift == 1, 1, jnp.where(shift == -2, 2, 3))))
        left = pool_ref[4, row_ref[k]]
        right = pool_ref[place, slot]
        half = jnp.dot(left, sum_ref[k], preferred_element_type=F32).astype(BF16)
        out_ref[k] = dot_nt(half, right).astype(BF16)
    for c in copies:
        c.wait()


def per_device(n_leaf, leaf_basis, transfer, transfer_top, coupling_parts, row_slot, col_node):
    any_ = pl.BlockSpec(memory_space=pl.ANY)
    vmem = pl.BlockSpec(memory_space=pltpu.VMEM)
    smem = pl.BlockSpec(memory_space=pltpu.SMEM)
    shape = jax.ShapeDtypeStruct
    dma = pltpu.SemaphoreType.DMA
    results = [
        shape((4, PTS, N), BF16),
        shape((7, N, N), F32),
        shape((2, 32, N), F32),
        shape((1, 32, N), F32),
    ]
    *outs, pool, summed = pl.pallas_call(
        functools.partial(main_kernel, n_leaf),
        out_shape=[*results, shape((5, 7, N, N), BF16), shape((16, N, N), BF16)],
        in_specs=[any_] * 4,
        out_specs=[any_] * 6,
        scratch_shapes=[
            pltpu.VMEM((4, PTS, N), BF16),
            pltpu.VMEM((7, N, N), F32),
            pltpu.VMEM((2, N, N), F32),
            pltpu.VMEM((7, N, N), F32),
            pltpu.VMEM((3, N, N), F32),
            pltpu.VMEM((4, N, N), F32),
            pltpu.VMEM((2, 8, N, N), BF16),
            pltpu.VMEM((2, 16, N, N), BF16),
            pltpu.VMEM((16, N, N), BF16),
            pltpu.VMEM((2, 8, N, N), BF16),
            pltpu.VMEM((7, N, N), BF16),
            pltpu.VMEM((4, PTS, N), BF16),
            pltpu.VMEM((7, N, N), F32),
            pltpu.VMEM((2, 32, N), F32),
            pltpu.VMEM((1, 32, N), F32),
            pltpu.VMEM((16, N, N), BF16),
            dma((6,)), dma((6,)), dma((6,)), dma((3,)), dma((3,)), dma((4,)), dma((4,)), dma((6,)),
        ],
        compiler_params=pltpu.CompilerParams(
            collective_id=0, has_side_effects=True, vmem_limit_bytes=40 << 20
        ),
        name="factor_and_send",
    )(leaf_basis, transfer, transfer_top, coupling_parts)
    coupling, *rest = pl.pallas_call(
        last_kernel,
        out_shape=[shape((16, N, N), BF16), *results],
        in_specs=[smem, smem, vmem, vmem] + [any_] * 4,
        out_specs=[vmem] + [any_] * 4,
        scratch_shapes=[dma((4,))],
        compiler_params=pltpu.CompilerParams(vmem_limit_bytes=40 << 20),
        name="project",
    )(row_slot, col_node, summed, pool, *outs)
    return (*rest, coupling)


def solution(mesh):
    lead = P(("leaf", "dom", "rep"), None, None)
    share = P(("leaf", "dom"), "rep", None)
    return jax.shard_map(
        functools.partial(per_device, mesh.shape["leaf"]),
        mesh=mesh,
        in_specs=(
            lead,
            lead,
            P(("leaf", "dom"), None, None),
            P("rep", ("leaf", "dom"), None, None),
            P(("leaf", "dom", "rep")),
            P(("leaf", "dom", "rep")),
        ),
        out_specs=(lead, lead, share, share, lead),
        check_vma=False,
    )
```

profile of v0, /device:TPU:30, one launch (start us, length us, event | category | flops | bytes accessed | tf_op | source)
XLA Modules:
  0.0 56.0 jit_solution(17638727413290951469)
XLA Ops:
  0.6 0.0 copy-start
  0.6 1.6 %copy-done = bf16[1,64,128,128]{3,2,1,0:T(8,128)(2,1)S(1)} copy-done((bf16[1,64,128,128]{3,2,1,0:T(8,128)(2,1)S(1)}, bf16[1,64,128,128]{3,2,1,0:T(8,128)(2,1)}, u32[]{:S(2)}) %copy-start) | copy-done | bytes 2097176
  2.2 0.0 copy-start.1
  2.2 1.0 %copy-done.1 = bf16[4,512,128]{2,1,0:T(8,128)(2,1)S(1)} copy-done((bf16[4,512,128]{2,1,0:T(8,128)(2,1)S(1)}, bf16[4,512,128]{2,1,0:T(8,128)(2,1)}, u32[]{:S(2)}) %copy-start.1) | copy-done | bytes 524312
  3.3 0.0 copy-start.2
  3.3 1.0 %copy-done.2 = f32[7,128,128]{2,1,0:T(8,128)S(1)} copy-done((f32[7,128,128]{2,1,0:T(8,128)S(1)}, f32[7,128,128]{2,1,0:T(8,128)}, u32[]{:S(2)}) %copy-start.2) | copy-done | bytes 458776
  4.3 0.0 copy-start.3
  4.3 0.9 %copy-done.3 = f32[2,128,128]{2,1,0:T(8,128)S(1)} copy-done((f32[2,128,128]{2,1,0:T(8,128)S(1)}, f32[2,128,128]{2,1,0:T(8,128)}, u32[]{:S(2)}) %copy-start.3) | copy-done | bytes 131096
  5.2 0.0 copy-start.4
  5.2 0.0 copy-start.5
  5.2 47.3 %factor_and_send.1 = (bf16[4,512,128]{2,1,0:T(8,128)(2,1)S(1)}, f32[7,128,128]{2,1,0:T(8,128)S(1)}, f32[2,32,128]{2,1,0:T(8,128)S(1)}, f32[1,32,128]{2,1,0:T(8,1...) custom-call(bf16[4,512,128]{2,1,0:T(8,128)(2,1)S(1)} %copy-done.1, ...), custom_call_target="tpu_custom_call" | custom-call | tf_op jit(solution)/shard_map/factor_and_send/pallas_call | solution.py:304
  52.5 0.0 copy-done.4
  52.5 0.0 copy-done.5
  52.5 3.3 %project.1 = (bf16[16,128,128]{2,1,0:T(8,128)(2,1)}, bf16[4,512,128]{2,1,0:T(8,128)(2,1)}, f32[7,128,128]{2,1,0:T(8,128)}, f32[2,32,128]{2,1,0:T(8,128)}, f32[1,32,128]{2,1,0:T(8,128)}) custom-call(s32[16]{0:T(128)S(1)} %copy-done.4, s32[16]{0:T(128)S(1)} %copy-done.5, bf16[16,128,128]{2,1,0:T(8,128)(2,1)S(1)} %get-tuple-element.16.sum_ref, ...), custom_call_target="tpu_custom_call" | custom-call | tf_op jit(solution)/shard_map/project/pallas_call | solution.py:333
Async XLA Ops:
  0.6 1.6 %copy-start = (bf16[1,64,128,128]{3,2,1,0:T(8,128)(2,1)S(1)}, bf16[1,64,128,128]{3,2,1,0:T(8,128)(2,1)}, u32[]{:S(2)}) copy-start(bf16[1,64,128,128]{3,2,1,0:T(8,128)(2,1)} %parts_hbm.1) | copy-start | bytes 6291460
  2.2 1.0 %copy-start.1 = (bf16[4,512,128]{2,1,0:T(8,128)(2,1)S(1)}, bf16[4,512,128]{2,1,0:T(8,128)(2,1)}, u32[]{:S(2)}) copy-start(bf16[4,512,128]{2,1,0:T(8,128)(2,1)} %leaf_hbm.1) | copy-start | bytes 1572868
  3.3 1.0 %copy-start.2 = (f32[7,128,128]{2,1,0:T(8,128)S(1)}, f32[7,128,128]{2,1,0:T(8,128)}, u32[]{:S(2)}) copy-start(f32[7,128,128]{2,1,0:T(8,128)} %trans_hbm.1) | copy-start | bytes 1376260
  4.3 0.9 %copy-start.3 = (f32[2,128,128]{2,1,0:T(8,128)S(1)}, f32[2,128,128]{2,1,0:T(8,128)}, u32[]{:S(2)}) copy-start(f32[2,128,128]{2,1,0:T(8,128)} %top_hbm.1) | copy-start | bytes 393220
  5.2 47.3 %copy-start.4 = (s32[16]{0:T(128)S(1)}, s32[16]{0:T(128)}, u32[]{:S(2)}) copy-start(s32[16]{0:T(128)} %row_ref.1) | copy-start | bytes 196
  5.2 47.3 %copy-start.5 = (s32[16]{0:T(128)S(1)}, s32[16]{0:T(128)}, u32[]{:S(2)}) copy-start(s32[16]{0:T(128)} %col_ref.1) | copy-start | bytes 196
where the time goes:
time: 56.3 us; the launch traced here: 56 us
  Pallas kernels  50.6 us (90%)
  local copies, waits for them, and re-layouts  4.55 us (8%)
  between operations  0.83 us (1%)
    pallas_call x1, Pallas kernels, per_device(): pl.pallas_call(functools.partial(main_kernel, n_leaf), out_shape=[*result...  47.3 us
    unnamed x12, local copies, waits for them, and re-layouts  4.55 us
    pallas_call x1, Pallas kernels, per_device(): pl.pallas_call(last_kernel, out_shape=[shape((16, N, N), BF16), *results]...  3.33 us

commit v1 on v0

v1 whole, which is shorter than its diff:
```python
import functools

import jax
import jax.numpy as jnp
from jax import lax
from jax.experimental import pallas as pl
from jax.experimental.pallas import tpu as pltpu
from jax.sharding import PartitionSpec as P

PTS = 512
N = 128
F32, BF16 = jnp.float32, jnp.bfloat16
MESH = pl.DeviceIdType.MESH
SWAP_AT = 4
PASS_AT = 7
TOPS_AT = 9
THROUGH_AT = 3
MAIN_VMEM = 60 << 20
LAST_VMEM = 60 << 20


def split3(x):
    high = x.astype(BF16)
    rest = x - high.astype(F32)
    mid = rest.astype(BF16)
    low = (rest - mid.astype(F32)).astype(BF16)
    return high, mid, low


def dot_tn(a, b):
    return lax.dot_general(a, b, (((0,), (0,)), ((), ())), preferred_element_type=F32)


def dot_nt(a, b):
    return lax.dot_general(a, b, (((1,), (1,)), ((), ())), preferred_element_type=F32)


def precise_tn(a, b):
    ah, am, al = split3(a)
    bh, bm, bl = split3(b)
    return dot_tn(
        jnp.concatenate([ah, ah, am, am, ah, al], 0),
        jnp.concatenate([bh, bm, bh, bm, bl, bh], 0),
    )


def precise_nn(a, b):
    return jnp.dot(a, b, precision=lax.Precision.HIGHEST, preferred_element_type=F32)


def precise_nt(a, b):
    return lax.dot_general(
        a, b, (((1,), (1,)), ((), ())), precision=lax.Precision.HIGHEST, preferred_element_type=F32
    )


def eliminate(m_ref, count, j):
    lane = lax.broadcasted_iota(jnp.int32, (1, 8, N), 2)
    sub = lax.broadcasted_iota(jnp.int32, (1, 8, N), 1)
    first = 8 * j
    rows = m_ref[:, first : first + 8, :]
    cols = [
        jnp.broadcast_to(rows[:, :, first + q : first + q + 1], (count, 8, N)) for q in range(8)
    ]
    inv = jnp.zeros((count, 8, N), F32)
    for q in range(8):
        r = 1.0 / cols[q][:, q : q + 1, :]
        inv = jnp.where(sub == q, r, inv)
        mult = jnp.where(sub > q, cols[q] * r, 0.0)
        for t in range(q + 1, 8):
            cols[t] = cols[t] - mult * cols[t][:, q : q + 1, :]
        rows = jnp.where(
            (lane == first + q) & (sub > q), -mult, rows - mult * rows[:, q : q + 1, :]
        )
    scale = jnp.sqrt(inv)
    done = rows * scale
    m_ref[:, first : first + 8, :] = done
    start = first + 8
    if start < N:
        row = first + sub
        ext = jnp.where(lane == row, scale, jnp.where((lane > row) & (lane < start), 0.0, done))
        lanes = lax.broadcasted_iota(jnp.int32, (N - start, N), 1)
        drop = (lanes >= first) & (lanes < start)
        for m in range(count):
            update = precise_tn(done[m], ext[m])[start:]
            m_ref[m, start:, :] = jnp.where(drop, 0.0, m_ref[m, start:, :]) - update


def upper(x):
    r = lax.broadcasted_iota(jnp.int32, (N, N), 0)
    c = lax.broadcasted_iota(jnp.int32, (N, N), 1)
    return jnp.where(c >= r, x, 0.0)


def lower_inverse(x):
    r = lax.broadcasted_iota(jnp.int32, (N, N), 0)
    c = lax.broadcasted_iota(jnp.int32, (N, N), 1)
    return jnp.where(c < r, x, jnp.where(c == r, 1.0 / x, 0.0))


def pack(ups):
    strips, halves = [], []
    for u in ups:
        strips.append(u[0:16])
        for i in (1, 2, 3):
            low = u[128 - 16 * i : 144 - 16 * i]
            strips.append(u[16 * i : 16 * i + 16] + pltpu.roll(low, 16 * i, 1))
        halves.append(u[64:80])
    for m in range(0, len(halves) - 1, 2):
        strips.append(halves[m] + pltpu.roll(halves[m + 1], 64, 1))
    if len(halves) % 2:
        strips.append(halves[-1])
    return strips


def main_kernel(
    n_leaf,
    row_ref, leaf_hbm, trans_hbm, top_hbm, parts_hbm,
    orth_hbm, new_hbm, ntop_hbm, ftop_hbm, pool_hbm, half_hbm,
    leaf_v, trans_v, top_v, mats, tops, c2, a_in, f_in, own, fwd, r_stack, packed,
    orth_v, new_v, ntop_v, ftop_v, half_v,
    in_sem, rs_send, rs_recv, g_send, g_recv, h_send, h_recv, out_sem,
):
    leaf, dom, rep = lax.axis_index("leaf"), lax.axis_index("dom"), lax.axis_index("rep")
    lin = (leaf * 2 + dom) * 4 + rep
    total = n_leaf * 8

    def linear(shift):
        t = lax.rem(lin + shift + total, total)
        return (lax.div(t, 8), lax.rem(lax.div(t, 4), 2), lax.rem(t, 4))

    def ring(shift):
        return lax.rem(rep + shift, 4)

    def ring_id(shift):
        return (leaf, dom, ring(shift))

    def load(src, dst, k):
        copy = pltpu.make_async_copy(src, dst, in_sem.at[k])
        copy.start()
        return copy

    barrier = pltpu.get_barrier_semaphore()
    for target in (ring_id(1), ring_id(3), linear(1), linear(-1)):
        pl.semaphore_signal(barrier, inc=1, device_id=target, device_id_type=MESH)

    load_leaf = load(leaf_hbm, leaf_v, 0)
    load_trans = load(trans_hbm, trans_v, 1)
    load_top = load(top_hbm, top_v, 2)
    load_own = load(parts_hbm.at[0, pl.ds(16 * rep, 16)], own, 3)
    load_fr = load(parts_hbm.at[0, pl.ds(16 * ring(1), 8)], fwd.at[0], 4)
    load_fl = load(parts_hbm.at[0, pl.ds(16 * ring(3) + 8, 8)], fwd.at[1], 5)
    pl.semaphore_wait(barrier, 4)

    def remote(src, dst, send, recv, target):
        copy = pltpu.make_async_remote_copy(
            src_ref=src, dst_ref=dst, send_sem=send, recv_sem=recv,
            device_id=target, device_id_type=MESH,
        )
        copy.start()
        return copy

    def block(dest, half):
        return parts_hbm.at[0, pl.ds(16 * ring(dest) + 8 * half, 8)]

    ar = remote(block(2, 0), a_in.at[0], rs_send.at[0], rs_recv.at[0], ring_id(1))
    al = remote(block(2, 1), a_in.at[1], rs_send.at[1], rs_recv.at[1], ring_id(3))

    load_leaf.wait()
    for i in range(4):
        u = leaf_v[i]
        mats[i] = dot_tn(u, u) * (1.0 / PTS)
    load_trans.wait()

    def lifted(g, e):
        return precise_tn(e, precise_tn(g, e))

    for p in range(2):
        mats[4 + p] = lifted(mats[2 * p], trans_v[2 * p]) + lifted(
            mats[2 * p + 1], trans_v[2 * p + 1]
        )
    mats[6] = lifted(mats[4], trans_v[4]) + lifted(mats[5], trans_v[5])
    c2[0] = lifted(mats[6], trans_v[6])
    low_bit = lax.rem(rep, 2)
    swaps = [
        remote(c2.at[0], c2.at[1], g_send.at[0], g_recv.at[0], (leaf, dom, rep + 1 - 2 * low_bit))
    ]
    br = remote(block(1, 1), f_in.at[0, pl.ds(8, 8)], rs_send.at[2], rs_recv.at[2], ring_id(1))
    bl = remote(block(3, 0), f_in.at[1, pl.ds(0, 8)], rs_send.at[3], rs_recv.at[3], ring_id(3))
    second = []

    def swap_pairs():
        swaps[0].wait_recv()
        c2[2] = c2[0] + c2[1]
        swaps.append(
            remote(c2.at[2], c2.at[3], g_send.at[1], g_recv.at[1], (leaf, dom, 3 - rep))
        )

    def pass_on():
        ar.wait_recv()
        load_fr.wait()
        for i in range(8):
            fwd[0, i] = (fwd[0, i].astype(F32) + a_in[0, i].astype(F32)).astype(BF16)
        second.append(
            remote(fwd.at[0], f_in.at[0, pl.ds(0, 8)], rs_send.at[4], rs_recv.at[4], ring_id(1))
        )
        al.wait_recv()
        load_fl.wait()
        for i in range(8):
            fwd[1, i] = (fwd[1, i].astype(F32) + a_in[1, i].astype(F32)).astype(BF16)
        second.append(
            remote(fwd.at[1], f_in.at[1, pl.ds(8, 8)], rs_send.at[5], rs_recv.at[5], ring_id(3))
        )

    first_half = rep < 2

    def top_grams():
        swaps[1].wait_recv()
        load_top.wait()
        first_node = jnp.where(first_half, c2[2], c2[3])
        second_node = jnp.where(first_half, c2[3], c2[2])
        tops[0] = first_node
        tops[1] = second_node
        tops[2] = lifted(first_node, top_v[0]) + lifted(second_node, top_v[1])

    for j in range(N // 8):
        if j == SWAP_AT:
            swap_pairs()
        if j == PASS_AT:
            pass_on()
        if j == TOPS_AT:
            top_grams()
        eliminate(mats, 7, j)
        if j >= TOPS_AT:
            eliminate(tops, 3, j - TOPS_AT)

    ups = [upper(mats[i]) for i in range(7)]
    for i, strip in enumerate(pack(ups)):
        packed[i] = strip.astype(BF16)
    halo = [
        remote(packed, pool_hbm.at[i], h_send.at[i], h_recv.at[i], linear(shift))
        for i, shift in enumerate((1, -1))
    ]
    for i in range(7):
        r_stack[i] = ups[i].astype(BF16)

    def store(src, dst, k):
        copy = pltpu.make_async_copy(src, dst, out_sem.at[k])
        copy.start()
        return copy

    stores = [store(packed, pool_hbm.at[4], 0)]

    def forward():
        for i, shift in enumerate((1, -1)):
            halo[i].wait_recv()
            halo.append(
                remote(pool_hbm.at[i], pool_hbm.at[2 + i], h_send.at[2 + i], h_recv.at[2 + i], linear(shift))
            )

    def sums():
        load_own.wait()
        for s in [br, bl, *second]:
            s.wait_recv()
        for i in range(16):
            total_i = own[i].astype(F32) + (f_in[0, i].astype(F32) + f_in[1, i].astype(F32))
            half_v[i] = jnp.dot(
                r_stack[row_ref[i]], total_i.astype(BF16), preferred_element_type=F32
            ).astype(BF16)
        stores.append(store(half_v, half_hbm, 5))

    for j in range(N // 8 - TOPS_AT, N // 8):
        eliminate(tops, 3, j)

    for i in range(4):
        orth_v[i] = dot_nt(leaf_v[i], lower_inverse(mats[i]).astype(BF16)).astype(BF16)
    stores.append(store(orth_v, orth_hbm, 1))
    for c in range(6):
        inverse = lower_inverse(mats[4 + c // 2])
        new_v[c] = precise_nt(precise_nn(upper(mats[c]), trans_v[c]), inverse)
    own_three = jnp.where(first_half, tops[0], tops[1])
    new_v[6] = precise_nt(precise_nn(upper(mats[6]), trans_v[6]), lower_inverse(own_three))
    stores.append(store(new_v, new_hbm, 2))
    top_inverse = lower_inverse(tops[2])
    share = pl.ds(pl.multiple_of(rep * 32, 32), 32)
    row = lax.broadcasted_iota(jnp.int32, (32, N), 0) + rep * 32
    col = lax.broadcasted_iota(jnp.int32, (32, N), 1)
    keep = col >= row
    for t in range(2):
        part = jnp.where(keep, tops[t, share, :], 0.0)
        ntop_v[t] = precise_nt(precise_nn(part, top_v[t]), top_inverse)
    ftop_v[0] = jnp.where(keep, tops[2, share, :], 0.0)
    stores.append(store(ntop_v, ntop_hbm, 3))
    stores.append(store(ftop_v, ftop_hbm, 4))

    forward()
    sums()
    for h in halo[2:]:
        h.wait_recv()
    for copy in [ar, al, br, bl, *swaps, *second, *halo]:
        copy.wait_send()
    for copy in stores:
        copy.wait()


def last_kernel(
    col_ref, half_hbm, pool_hbm, orth_in, new_in, ntop_in, ftop_in,
    out_hbm, orth_out, new_out, ntop_out, ftop_out,
    half_ref, pool_ref, orth_v, new_v, ntop_v, ftop_v, out_v, in_sems, sems,
):
    loads = [
        pltpu.make_async_copy(a, b, in_sems.at[i])
        for i, (a, b) in enumerate(
            (
                (half_hbm, half_ref), (pool_hbm, pool_ref),
                (orth_in, orth_v), (new_in, new_v), (ntop_in, ntop_v), (ftop_in, ftop_v),
            )
        )
    ]
    for c in loads:
        c.start()
    for c in loads[:2]:
        c.wait()
    copies = []

    def through():
        for i, (a, b) in enumerate(
            ((orth_v, orth_out), (new_v, new_out), (ntop_v, ntop_out), (ftop_v, ftop_out))
        ):
            loads[2 + i].wait()
            c = pltpu.make_async_copy(a, b, sems.at[i])
            c.start()
            copies.append(c)

    me = (lax.axis_index("leaf") * 2 + lax.axis_index("dom")) * 4 + lax.axis_index("rep")
    lane = lax.broadcasted_iota(jnp.int32, (16, N), 1)

    def keep(x, first):
        return jnp.where(lane >= first, x, 0.0)

    for k in range(16):
        node = col_ref[k]
        device = lax.div(node, 7)
        slot = node - 7 * device
        shift = device - me
        place = jnp.where(
            shift == 0, 4, jnp.where(shift > 0, 2 * shift - 1, -2 * shift - 2)
        )
        strip = [pool_ref[place, 4 * slot + i].astype(F32) for i in range(4)]
        pair = pool_ref[place, 28 + lax.div(slot, 2)].astype(F32)
        pair = jnp.where(lax.rem(slot, 2) == 1, pltpu.roll(pair, 64, 1), pair)
        right = jnp.concatenate(
            [strip[0]]
            + [keep(strip[i], 16 * i) for i in (1, 2, 3)]
            + [keep(pair, 64)]
            + [keep(pltpu.roll(strip[i], N - 16 * i, 1), N - 16 * i) for i in (3, 2, 1)],
            0,
        ).astype(BF16)
        out_v[k] = dot_nt(half_ref[k], right).astype(BF16)
        if k % 4 == 3:
            part = pl.ds(k - 3, 4)
            c = pltpu.make_async_copy(out_v.at[part], out_hbm.at[part], sems.at[4 + k // 4])
            c.start()
            copies.append(c)
        if k == THROUGH_AT:
            through()
    for c in copies:
        c.wait()


def per_device(n_leaf, leaf_basis, transfer, transfer_top, coupling_parts, row_slot, col_node):
    any_ = pl.BlockSpec(memory_space=pl.ANY)
    smem = pl.BlockSpec(memory_space=pltpu.SMEM)
    shape = jax.ShapeDtypeStruct
    dma = pltpu.SemaphoreType.DMA
    results = [
        shape((4, PTS, N), BF16),
        shape((7, N, N), F32),
        shape((2, 32, N), F32),
        shape((1, 32, N), F32),
    ]
    *outs, pool, half = pl.pallas_call(
        functools.partial(main_kernel, n_leaf),
        out_shape=[*results, shape((5, 32, 16, N), BF16), shape((16, N, N), BF16)],
        in_specs=[smem] + [any_] * 4,
        out_specs=[any_] * 6,
        scratch_shapes=[
            pltpu.VMEM((4, PTS, N), BF16),
            pltpu.VMEM((7, N, N), F32),
            pltpu.VMEM((2, N, N), F32),
            pltpu.VMEM((7, N, N), F32),
            pltpu.VMEM((3, N, N), F32),
            pltpu.VMEM((4, N, N), F32),
            pltpu.VMEM((2, 8, N, N), BF16),
            pltpu.VMEM((2, 16, N, N), BF16),
            pltpu.VMEM((16, N, N), BF16),
            pltpu.VMEM((2, 8, N, N), BF16),
            pltpu.VMEM((7, N, N), BF16),
            pltpu.VMEM((32, 16, N), BF16),
            pltpu.VMEM((4, PTS, N), BF16),
            pltpu.VMEM((7, N, N), F32),
            pltpu.VMEM((2, 32, N), F32),
            pltpu.VMEM((1, 32, N), F32),
            pltpu.VMEM((16, N, N), BF16),
            dma((6,)), dma((6,)), dma((6,)), dma((2,)), dma((2,)), dma((4,)), dma((4,)), dma((6,)),
        ],
        compiler_params=pltpu.CompilerParams(
            collective_id=0, has_side_effects=True, vmem_limit_bytes=MAIN_VMEM
        ),
        name="factor_and_send",
    )(row_slot, leaf_basis, transfer, transfer_top, coupling_parts)
    coupling, *rest = pl.pallas_call(
        last_kernel,
        out_shape=[shape((16, N, N), BF16), *results],
        in_specs=[smem] + [any_] * 6,
        out_specs=[any_] * 5,
        scratch_shapes=[
            pltpu.VMEM((16, N, N), BF16),
            pltpu.VMEM((5, 32, 16, N), BF16),
            pltpu.VMEM((4, PTS, N), BF16),
            pltpu.VMEM((7, N, N), F32),
            pltpu.VMEM((2, 32, N), F32),
            pltpu.VMEM((1, 32, N), F32),
            pltpu.VMEM((16, N, N), BF16),
            dma((6,)),
            dma((8,)),
        ],
        compiler_params=pltpu.CompilerParams(vmem_limit_bytes=LAST_VMEM),
        name="project",
    )(col_node, half, pool, *outs)
    return (*rest, coupling)


def solution(mesh):
    lead = P(("leaf", "dom", "rep"), None, None)
    share = P(("leaf", "dom"), "rep", None)
    return jax.shard_map(
        functools.partial(per_device, mesh.shape["leaf"]),
        mesh=mesh,
        in_specs=(
            lead,
            lead,
            P(("leaf", "dom"), None, None),
            P("rep", ("leaf", "dom"), None, None),
            P(("leaf", "dom", "rep")),
            P(("leaf", "dom", "rep")),
        ),
        out_specs=(lead, lead, share, share, lead),
        check_vma=False,
    )
```

time: 56.3 us -> 48.9 us (0.87)
  the two profiles are of different devices: /device:TPU:30 before, /device:TPU:1 now
where the time goes in v1:
time: 48.9 us; the launch traced here: 48.8 us
  Pallas kernels  48.1 us (98%)
  between operations  0.64 us (1%)
    pallas_call x1, Pallas kernels, per_device(): pl.pallas_call(functools.partial(main_kernel, n_leaf), out_shape=[*result...  44.7 us
    pallas_call x1, Pallas kernels, per_device(): pl.pallas_call(last_kernel, out_shape=[shape((16, N, N), BF16), *results]...  3.46 us

profile of v1, /device:TPU:1, one launch (start us, length us, event | category | flops | bytes accessed | tf_op | source)
XLA Modules:
  0.0 48.8 jit_solution(13087918885074098341)
XLA Ops:
  0.6 44.7 %factor_and_send.1 = (bf16[4,512,128]{2,1,0:T(8,128)(2,1)}, f32[7,128,128]{2,1,0:T(8,128)}, f32[2,32,128]{2,1,0:T(8,128)}, f32[1,32,128]{2,1,0:T(8,128)}, bf16[5...) custom-call(s32[16]{0:T(128)} %row_ref.1, bf16[4,512,128]{2,1,0:T(8,128)(2,1)} %leaf_hbm.1, ...), custom_call_target="tpu_custom_call" | custom-call | tf_op jit(solution)/shard_map/factor_and_send/pallas_call | solution.py:382
  45.3 3.5 %project.1 = (bf16[16,128,128]{2,1,0:T(8,128)(2,1)}, bf16[4,512,128]{2,1,0:T(8,128)(2,1)}, f32[7,128,128]{2,1,0:T(8,128)}, f32[2,32,128]{2,1,0:T(8,128)}, f32[1,32,128]{2,1,0:T(8,128)}) custom-call(s32[16]{0:T(128)} %col_ref.1, bf16[16,128,128]{2,1,0:T(8,128)(2,1)} %get-tuple-element.16.half_hbm, bf16[5,32,16,128]{3,2,1,0:T(8,128)(2,1)} %get-tuple-element.17.pool_hbm, ...), custom_call_target="tpu_custom_call" | custom-call | tf_op jit(solution)/shard_map/project/pallas_call | solution.py:412

commit v2 on v1

--- a/solution.py
+++ b/solution.py
@@ -12,9 +12,12 @@
 F32, BF16 = jnp.float32, jnp.bfloat16
 MESH = pl.DeviceIdType.MESH
 SWAP_AT = 4
-PASS_AT = 7
+PASS_AT = 8
+DIRECT_AT = 16
 TOPS_AT = 9
 THROUGH_AT = 3
+FORWARD_AT = 16
+EARLY = 1
 MAIN_VMEM = 60 << 20
 LAST_VMEM = 60 << 20
 
@@ -119,7 +122,7 @@
     orth_hbm, new_hbm, ntop_hbm, ftop_hbm, pool_hbm, half_hbm,
     leaf_v, trans_v, top_v, mats, tops, c2, a_in, f_in, own, fwd, r_stack, packed,
     orth_v, new_v, ntop_v, ftop_v, half_v,
-    in_sem, rs_send, rs_recv, g_send, g_recv, h_send, h_recv, out_sem,
+    in_sem, rs_send, rs_recv, g_send, g_recv, h_send, h_recv, out_sem, hello,
 ):
     leaf, dom, rep = lax.axis_index("leaf"), lax.axis_index("dom"), lax.axis_index("rep")
     lin = (leaf * 2 + dom) * 4 + rep
@@ -141,8 +144,12 @@
         return copy
 
     barrier = pltpu.get_barrier_semaphore()
-    for target in (ring_id(1), ring_id(3), linear(1), linear(-1)):
+    for target in (ring_id(1), ring_id(3)):
         pl.semaphore_signal(barrier, inc=1, device_id=target, device_id_type=MESH)
+
+    @pl.when(rep == 0)
+    def _():
+        pl.semaphore_signal(barrier, inc=1, device_id=linear(-1), device_id_type=MESH)
 
     load_leaf = load(leaf_hbm, leaf_v, 0)
     load_trans = load(trans_hbm, trans_v, 1)
@@ -150,7 +157,35 @@
     load_own = load(parts_hbm.at[0, pl.ds(16 * rep, 16)], own, 3)
     load_fr = load(parts_hbm.at[0, pl.ds(16 * ring(1), 8)], fwd.at[0], 4)
     load_fl = load(parts_hbm.at[0, pl.ds(16 * ring(3) + 8, 8)], fwd.at[1], 5)
-    pl.semaphore_wait(barrier, 4)
+
+    def lifted(g, e):
+        return precise_tn(e, precise_tn(g, e))
+
+    def leaf_grams():
+        load_leaf.wait()
+        for i in range(4):
+            u = leaf_v[i]
+            mats[i] = dot_tn(u, u) * (1.0 / PTS)
+        load_trans.wait()
+
+    def first_level():
+        for p in range(2):
+            mats[4 + p] = lifted(mats[2 * p], trans_v[2 * p]) + lifted(
+                mats[2 * p + 1], trans_v[2 * p + 1]
+            )
+
+    def second_level():
+        mats[6] = lifted(mats[4], trans_v[4]) + lifted(mats[5], trans_v[5])
+        c2[0] = lifted(mats[6], trans_v[6])
+
+    grams = [leaf_grams, first_level, second_level]
+    for g in grams[:EARLY]:
+        g()
+    pl.semaphore_wait(barrier, 2 + lax.div(rep, 3))
+
+    @pl.when(rep == 3)
+    def _():
+        pl.semaphore_signal(hello, inc=1, device_id=linear(1), device_id_type=MESH)
 
     def remote(src, dst, send, recv, target):
         copy = pltpu.make_async_remote_copy(
@@ -166,27 +201,24 @@
     ar = remote(block(2, 0), a_in.at[0], rs_send.at[0], rs_recv.at[0], ring_id(1))
     al = remote(block(2, 1), a_in.at[1], rs_send.at[1], rs_recv.at[1], ring_id(3))
 
-    load_leaf.wait()
-    for i in range(4):
-        u = leaf_v[i]
-        mats[i] = dot_tn(u, u) * (1.0 / PTS)
-    load_trans.wait()
-
-    def lifted(g, e):
-        return precise_tn(e, precise_tn(g, e))
-
-    for p in range(2):
-        mats[4 + p] = lifted(mats[2 * p], trans_v[2 * p]) + lifted(
-            mats[2 * p + 1], trans_v[2 * p + 1]
-        )
-    mats[6] = lifted(mats[4], trans_v[4]) + lifted(mats[5], trans_v[5])
-    c2[0] = lifted(mats[6], trans_v[6])
+    for g in grams[EARLY:]:
+        g()
     low_bit = lax.rem(rep, 2)
     swaps = [
         remote(c2.at[0], c2.at[1], g_send.at[0], g_recv.at[0], (leaf, dom, rep + 1 - 2 * low_bit))
     ]
-    br = remote(block(1, 1), f_in.at[0, pl.ds(8, 8)], rs_send.at[2], rs_recv.at[2], ring_id(1))
-    bl = remote(block(3, 0), f_in.at[1, pl.ds(0, 8)], rs_send.at[3], rs_recv.at[3], ring_id(3))
+    direct = []
+
+    def send_direct():
+        direct.append(
+            remote(block(1, 1), f_in.at[0, pl.ds(8, 8)], rs_send.at[2], rs_recv.at[2], ring_id(1))
+        )
+        direct.append(
+            remote(block(3, 0), f_in.at[1, pl.ds(0, 8)], rs_send.at[3], rs_recv.at[3], ring_id(3))
+        )
+
+    if DIRECT_AT == -1:
+        send_direct()
     second = []
 
     def swap_pairs():
@@ -230,6 +262,8 @@
             pass_on()
         if j == TOPS_AT:
             top_grams()
+        if j == DIRECT_AT:
+            send_direct()
         eliminate(mats, 7, j)
         if j >= TOPS_AT:
             eliminate(tops, 3, j - TOPS_AT)
@@ -237,10 +271,17 @@
     ups = [upper(mats[i]) for i in range(7)]
     for i, strip in enumerate(pack(ups)):
         packed[i] = strip.astype(BF16)
+
+    @pl.when(rep == 0)
+    def _():
+        pl.semaphore_wait(hello, 1)
+
     halo = [
         remote(packed, pool_hbm.at[i], h_send.at[i], h_recv.at[i], linear(shift))
         for i, shift in enumerate((1, -1))
     ]
+    if DIRECT_AT == 16:
+        send_direct()
     for i in range(7):
         r_stack[i] = ups[i].astype(BF16)
 
@@ -260,7 +301,7 @@
 
     def sums():
         load_own.wait()
-        for s in [br, bl, *second]:
+        for s in [*direct, *second]:
             s.wait_recv()
         for i in range(16):
             total_i = own[i].astype(F32) + (f_in[0, i].astype(F32) + f_in[1, i].astype(F32))
@@ -270,7 +311,11 @@
         stores.append(store(half_v, half_hbm, 5))
 
     for j in range(N // 8 - TOPS_AT, N // 8):
+        if j == FORWARD_AT:
+            forward()
         eliminate(tops, 3, j)
+    if FORWARD_AT == 16:
+        forward()
 
     for i in range(4):
         orth_v[i] = dot_nt(leaf_v[i], lower_inverse(mats[i]).astype(BF16)).astype(BF16)
@@ -293,11 +338,12 @@
     stores.append(store(ntop_v, ntop_hbm, 3))
     stores.append(store(ftop_v, ftop_hbm, 4))
 
-    forward()
+    if FORWARD_AT == 17:
+        forward()
     sums()
     for h in halo[2:]:
         h.wait_recv()
-    for copy in [ar, al, br, bl, *swaps, *second, *halo]:
+    for copy in [ar, al, *direct, *swaps, *second, *halo]:
         copy.wait_send()
     for copy in stores:
         copy.wait()
@@ -403,6 +449,7 @@
             pltpu.VMEM((1, 32, N), F32),
             pltpu.VMEM((16, N, N), BF16),
             dma((6,)), dma((6,)), dma((6,)), dma((2,)), dma((2,)), dma((4,)), dma((4,)), dma((6,)),
+            pltpu.SemaphoreType.REGULAR,
         ],
         compiler_params=pltpu.CompilerParams(
             collective_id=0, has_side_effects=True, vmem_limit_bytes=MAIN_VMEM

time: 48.9 us -> 43.6 us (0.89)
  the two profiles are of different devices: /device:TPU:1 before, /device:TPU:2 now
where the time goes in v2:
time: 43.6 us; the launch traced here: 43.4 us
  Pallas kernels  42.6 us (98%)
  between operations  0.8 us (2%)
    pallas_call x1, Pallas kernels, per_device(): pl.pallas_call(functools.partial(main_kernel, n_leaf), out_shape=[*result...  39.2 us
    pallas_call x1, Pallas kernels, per_device(): pl.pallas_call(last_kernel, out_shape=[shape((16, N, N), BF16), *results]...  3.45 us

profile of v2, /device:TPU:2, one launch (start us, length us, event | category | flops | bytes accessed | tf_op | source)
XLA Modules:
  0.0 43.4 jit_solution(8474422111022187073)
XLA Ops:
  0.6 39.2 %factor_and_send.1 = (bf16[4,512,128]{2,1,0:T(8,128)(2,1)}, f32[7,128,128]{2,1,0:T(8,128)}, f32[2,32,128]{2,1,0:T(8,128)}, f32[1,32,128]{2,1,0:T(8,128)}, bf16[5...) custom-call(s32[16]{0:T(128)} %row_ref.1, bf16[4,512,128]{2,1,0:T(8,128)(2,1)} %leaf_hbm.1, ...), custom_call_target="tpu_custom_call" | custom-call | tf_op jit(solution)/shard_map/factor_and_send/pallas_call | solution.py:428
  39.8 3.5 %project.1 = (bf16[16,128,128]{2,1,0:T(8,128)(2,1)}, bf16[4,512,128]{2,1,0:T(8,128)(2,1)}, f32[7,128,128]{2,1,0:T(8,128)}, f32[2,32,128]{2,1,0:T(8,128)}, f32[1,32,128]{2,1,0:T(8,128)}) custom-call(s32[16]{0:T(128)} %col_ref.1, bf16[16,128,128]{2,1,0:T(8,128)(2,1)} %get-tuple-element.16.half_hbm, bf16[5,32,16,128]{3,2,1,0:T(8,128)(2,1)} %get-tuple-element.17.pool_hbm, ...), custom_call_target="tpu_custom_call" | custom-call | tf_op jit(solution)/shard_map/project/pallas_call | solution.py:459

commit v3 on v2

--- a/solution.py
+++ b/solution.py
@@ -12,14 +12,12 @@
 F32, BF16 = jnp.float32, jnp.bfloat16
 MESH = pl.DeviceIdType.MESH
 SWAP_AT = 4
-PASS_AT = 8
-DIRECT_AT = 16
+PASS_AT = 7
 TOPS_AT = 9
-THROUGH_AT = 3
 FORWARD_AT = 16
 EARLY = 1
-MAIN_VMEM = 60 << 20
-LAST_VMEM = 60 << 20
+MAIN_VMEM = 54 << 20
+LAST_VMEM = 1 << 20
 
 
 def split3(x):
@@ -118,10 +116,10 @@
 
 def main_kernel(
     n_leaf,
-    row_ref, leaf_hbm, trans_hbm, top_hbm, parts_hbm,
-    orth_hbm, new_hbm, ntop_hbm, ftop_hbm, pool_hbm, half_hbm,
-    leaf_v, trans_v, top_v, mats, tops, c2, a_in, f_in, own, fwd, r_stack, packed,
-    orth_v, new_v, ntop_v, ftop_v, half_v,
+    row_ref, col_ref, leaf_hbm, trans_hbm, top_hbm, parts_hbm,
+    orth_hbm, new_hbm, ntop_hbm, ftop_hbm, coup_hbm,
+    leaf_v, trans_v, top_v, mats, tops, c2, a_in, f_in, own, fwd, r_stack, pool,
+    orth_v, new_v, ntop_v, ftop_v, half_v, coup_v,
     in_sem, rs_send, rs_recv, g_send, g_recv, h_send, h_recv, out_sem, hello,
 ):
     leaf, dom, rep = lax.axis_index("leaf"), lax.axis_index("dom"), lax.axis_index("rep")
@@ -210,15 +208,17 @@
     direct = []
 
     def send_direct():
-        direct.append(
-            remote(block(1, 1), f_in.at[0, pl.ds(8, 8)], rs_send.at[2], rs_recv.at[2], ring_id(1))
-        )
-        direct.append(
-            remote(block(3, 0), f_in.at[1, pl.ds(0, 8)], rs_send.at[3], rs_recv.at[3], ring_id(3))
-        )
-
-    if DIRECT_AT == -1:
-        send_direct()
+        for part in range(2):
+            for side, (dest, first, k) in enumerate(((1, 8, 2), (3, 0, 3))):
+                rows = pl.ds(first + 4 * part, 4)
+                k += 4 * part
+                direct.append(
+                    remote(
+                        parts_hbm.at[0, pl.ds(16 * ring(dest) + first + 4 * part, 4)],
+                        f_in.at[side, rows], rs_send.at[k], rs_recv.at[k], ring_id(dest),
+                    )
+                )
+
     second = []
 
     def swap_pairs():
@@ -262,26 +262,23 @@
             pass_on()
         if j == TOPS_AT:
             top_grams()
-        if j == DIRECT_AT:
-            send_direct()
         eliminate(mats, 7, j)
         if j >= TOPS_AT:
             eliminate(tops, 3, j - TOPS_AT)
 
     ups = [upper(mats[i]) for i in range(7)]
     for i, strip in enumerate(pack(ups)):
-        packed[i] = strip.astype(BF16)
+        pool[2, i] = strip.astype(BF16)
 
     @pl.when(rep == 0)
     def _():
         pl.semaphore_wait(hello, 1)
 
     halo = [
-        remote(packed, pool_hbm.at[i], h_send.at[i], h_recv.at[i], linear(shift))
+        remote(pool.at[2], pool.at[1 + 2 * i], h_send.at[i], h_recv.at[i], linear(shift))
         for i, shift in enumerate((1, -1))
     ]
-    if DIRECT_AT == 16:
-        send_direct()
+    send_direct()
     for i in range(7):
         r_stack[i] = ups[i].astype(BF16)
 
@@ -290,25 +287,53 @@
         copy.start()
         return copy
 
-    stores = [store(packed, pool_hbm.at[4], 0)]
+    stores = []
 
     def forward():
         for i, shift in enumerate((1, -1)):
             halo[i].wait_recv()
             halo.append(
-                remote(pool_hbm.at[i], pool_hbm.at[2 + i], h_send.at[2 + i], h_recv.at[2 + i], linear(shift))
+                remote(pool.at[1 + 2 * i], pool.at[4 * i], h_send.at[2 + i], h_recv.at[2 + i], linear(shift))
             )
 
-    def sums():
+    def halve(i):
+        total_i = own[i].astype(F32) + (f_in[0, i].astype(F32) + f_in[1, i].astype(F32))
+        return jnp.dot(
+            r_stack[row_ref[i]], total_i.astype(BF16), preferred_element_type=F32
+        ).astype(BF16)
+
+    def project():
         load_own.wait()
-        for s in [*direct, *second]:
+        for s in [*second, *direct]:
             s.wait_recv()
         for i in range(16):
-            total_i = own[i].astype(F32) + (f_in[0, i].astype(F32) + f_in[1, i].astype(F32))
-            half_v[i] = jnp.dot(
-                r_stack[row_ref[i]], total_i.astype(BF16), preferred_element_type=F32
+            half_v[i] = halve(i)
+        for h in halo[2:]:
+            h.wait_recv()
+        lane = lax.broadcasted_iota(jnp.int32, (16, N), 1)
+
+        def keep_from(x, first):
+            return jnp.where(lane >= first, x, 0.0)
+
+        for k in range(16):
+            node = jnp.minimum(jnp.maximum(col_ref[k] - 7 * lin + 14, 0), 34)
+            place = sum(jnp.where(node >= 7 * d, 1, 0) for d in (1, 2, 3, 4))
+            slot = node - 7 * place
+            half_slot = sum(jnp.where(slot >= d, 1, 0) for d in (2, 4, 6))
+            strip = [pool[place, 4 * slot + i].astype(F32) for i in range(4)]
+            pair = pool[place, 28 + half_slot].astype(F32)
+            pair = jnp.where(slot - 2 * half_slot == 1, pltpu.roll(pair, 64, 1), pair)
+            right = jnp.concatenate(
+                [strip[0]]
+                + [keep_from(strip[i], 16 * i) for i in (1, 2, 3)]
+                + [keep_from(pair, 64)]
+                + [keep_from(pltpu.roll(strip[i], N - 16 * i, 1), N - 16 * i) for i in (3, 2, 1)],
+                0,
             ).astype(BF16)
-        stores.append(store(half_v, half_hbm, 5))
+            coup_v[k] = dot_nt(half_v[k], right).astype(BF16)
+            if k % 8 == 7:
+                part = pl.ds(k - 7, 8)
+                stores.append(store(coup_v.at[part], coup_hbm.at[part], 5 + k // 8))
 
     for j in range(N // 8 - TOPS_AT, N // 8):
         if j == FORWARD_AT:
@@ -338,78 +363,18 @@
     stores.append(store(ntop_v, ntop_hbm, 3))
     stores.append(store(ftop_v, ftop_hbm, 4))
 
-    if FORWARD_AT == 17:
-        forward()
-    sums()
-    for h in halo[2:]:
-        h.wait_recv()
+    project()
     for copy in [ar, al, *direct, *swaps, *second, *halo]:
         copy.wait_send()
     for copy in stores:
         copy.wait()
 
 
-def last_kernel(
-    col_ref, half_hbm, pool_hbm, orth_in, new_in, ntop_in, ftop_in,
-    out_hbm, orth_out, new_out, ntop_out, ftop_out,
-    half_ref, pool_ref, orth_v, new_v, ntop_v, ftop_v, out_v, in_sems, sems,
-):
-    loads = [
-        pltpu.make_async_copy(a, b, in_sems.at[i])
-        for i, (a, b) in enumerate(
-            (
-                (half_hbm, half_ref), (pool_hbm, pool_ref),
-                (orth_in, orth_v), (new_in, new_v), (ntop_in, ntop_v), (ftop_in, ftop_v),
-            )
-        )
-    ]
-    for c in loads:
+def last_kernel(*refs):
+    ins, outs, sems = refs[:5], refs[5:10], refs[10]
+    copies = [pltpu.make_async_copy(a, b, sems.at[i]) for i, (a, b) in enumerate(zip(ins, outs))]
+    for c in copies:
         c.start()
-    for c in loads[:2]:
-        c.wait()
-    copies = []
-
-    def through():
-        for i, (a, b) in enumerate(
-            ((orth_v, orth_out), (new_v, new_out), (ntop_v, ntop_out), (ftop_v, ftop_out))
-        ):
-            loads[2 + i].wait()
-            c = pltpu.make_async_copy(a, b, sems.at[i])
-            c.start()
-            copies.append(c)
-
-    me = (lax.axis_index("leaf") * 2 + lax.axis_index("dom")) * 4 + lax.axis_index("rep")
-    lane = lax.broadcasted_iota(jnp.int32, (16, N), 1)
-
-    def keep(x, first):
-        return jnp.where(lane >= first, x, 0.0)
-
-    for k in range(16):
-        node = col_ref[k]
-        device = lax.div(node, 7)
-        slot = node - 7 * device
-        shift = device - me
-        place = jnp.where(
-            shift == 0, 4, jnp.where(shift > 0, 2 * shift - 1, -2 * shift - 2)
-        )
-        strip = [pool_ref[place, 4 * slot + i].astype(F32) for i in range(4)]
-        pair = pool_ref[place, 28 + lax.div(slot, 2)].astype(F32)
-        pair = jnp.where(lax.rem(slot, 2) == 1, pltpu.roll(pair, 64, 1), pair)
-        right = jnp.concatenate(
-            [strip[0]]
-            + [keep(strip[i], 16 * i) for i in (1, 2, 3)]
-            + [keep(pair, 64)]
-            + [keep(pltpu.roll(strip[i], N - 16 * i, 1), N - 16 * i) for i in (3, 2, 1)],
-            0,
-        ).astype(BF16)
-        out_v[k] = dot_nt(half_ref[k], right).astype(BF16)
-        if k % 4 == 3:
-            part = pl.ds(k - 3, 4)
-            c = pltpu.make_async_copy(out_v.at[part], out_hbm.at[part], sems.at[4 + k // 4])
-            c.start()
-            copies.append(c)
-        if k == THROUGH_AT:
-            through()
     for c in copies:
         c.wait()
 
@@ -424,12 +389,13 @@
         shape((7, N, N), F32),
         shape((2, 32, N), F32),
         shape((1, 32, N), F32),
+        shape((16, N, N), BF16),
     ]
-    *outs, pool, half = pl.pallas_call(
+    outs = pl.pallas_call(
         functools.partial(main_kernel, n_leaf),
-        out_shape=[*results, shape((5, 32, 16, N), BF16), shape((16, N, N), BF16)],
-        in_specs=[smem] + [any_] * 4,
-        out_specs=[any_] * 6,
+        out_shape=[pltpu.VMEM(r.shape, r.dtype) for r in results],
+        in_specs=[smem] * 2 + [any_] * 4,
+        out_specs=[any_] * 5,
         scratch_shapes=[
             pltpu.VMEM((4, PTS, N), BF16),
             pltpu.VMEM((7, N, N), F32),
@@ -442,40 +408,30 @@
             pltpu.VMEM((16, N, N), BF16),
             pltpu.VMEM((2, 8, N, N), BF16),
             pltpu.VMEM((7, N, N), BF16),
-            pltpu.VMEM((32, 16, N), BF16),
+            pltpu.VMEM((5, 32, 16, N), BF16),
             pltpu.VMEM((4, PTS, N), BF16),
             pltpu.VMEM((7, N, N), F32),
             pltpu.VMEM((2, 32, N), F32),
             pltpu.VMEM((1, 32, N), F32),
             pltpu.VMEM((16, N, N), BF16),
-            dma((6,)), dma((6,)), dma((6,)), dma((2,)), dma((2,)), dma((4,)), dma((4,)), dma((6,)),
+            pltpu.VMEM((16, N, N), BF16),
+            dma((6,)), dma((8,)), dma((8,)), dma((2,)), dma((2,)), dma((4,)), dma((4,)), dma((7,)),
             pltpu.SemaphoreType.REGULAR,
         ],
         compiler_params=pltpu.CompilerParams(
             collective_id=0, has_side_effects=True, vmem_limit_bytes=MAIN_VMEM
         ),
         name="factor_and_send",
-    )(row_slot, leaf_basis, transfer, transfer_top, coupling_parts)
-    coupling, *rest = pl.pallas_call(
+    )(row_slot, col_node, leaf_basis, transfer, transfer_top, coupling_parts)
+    return pl.pallas_call(
         last_kernel,
-        out_shape=[shape((16, N, N), BF16), *results],
-        in_specs=[smem] + [any_] * 6,
+        out_shape=results,
+        in_specs=[any_] * 5,
         out_specs=[any_] * 5,
-        scratch_shapes=[
-            pltpu.VMEM((16, N, N), BF16),
-            pltpu.VMEM((5, 32, 16, N), BF16),
-            pltpu.VMEM((4, PTS, N), BF16),
-            pltpu.VMEM((7, N, N), F32),
-            pltpu.VMEM((2, 32, N), F32),
-            pltpu.VMEM((1, 32, N), F32),
-            pltpu.VMEM((16, N, N), BF16),
-            dma((6,)),
-            dma((8,)),
-        ],
+        scratch_shapes=[dma((5,))],
         compiler_params=pltpu.CompilerParams(vmem_limit_bytes=LAST_VMEM),
-        name="project",
-    )(col_node, half, pool, *outs)
-    return (*rest, coupling)
+        name="hand_over",
+    )(*outs)
 
 
 def solution(mesh):

time: 43.6 us -> 41.8 us (0.959)
  Pallas kernels: 42.6 us -> 40.8 us
    pallas_call x2, Pallas kernels: 42.6 us -> 40.8 us  [the longest x1 39.7 us: per_device(): pl.pallas_call(functools.partial(main_kernel, n_leaf), out_shape=[pltpu.V...]
where the time goes in v3:
time: 41.8 us; the launch traced here: 41.6 us
  Pallas kernels  40.8 us (98%)
  between operations  0.8 us (2%)
    pallas_call x1, Pallas kernels, per_device(): pl.pallas_call(functools.partial(main_kernel, n_leaf), out_shape=[pltpu.V...  39.7 us
    pallas_call x1, Pallas kernels, per_device(): pl.pallas_call(last_kernel, out_shape=results, in_specs=[any_] * 5, out_s...  1.18 us

profile of v3, /device:TPU:2, one launch (start us, length us, event | category | flops | bytes accessed | tf_op | source)
XLA Modules:
  0.0 41.6 jit_solution(1629687742218360251)
XLA Ops:
  0.6 39.7 %factor_and_send.1 = (bf16[4,512,128]{2,1,0:T(8,128)(2,1)S(1)}, f32[7,128,128]{2,1,0:T(8,128)S(1)}, f32[2,32,128]{2,1,0:T(8,128)S(1)}, f32[1,32,128]{2,1,0:T(8,128)S(1)}, bf16[16,128,128]{2,1,0:T(8,128)(2,1)S(1)}) custom-call(s32[16]{0:T(128)} %row_ref.1, s32[16]{0:T(128)} %col_ref.1, bf16[4,512,128]{2,1,0:T(8,128)(2,1)} %leaf_hbm.1, ...), custom_call_target="tpu_custom_call" | custom-call | tf_op jit(solution)/shard_map/factor_and_send/pallas_call | solution.py:394
  40.3 1.2 %hand_over.1 = (bf16[4,512,128]{2,1,0:T(8,128)(2,1)}, f32[7,128,128]{2,1,0:T(8,128)}, f32[2,32,128]{2,1,0:T(8,128)}, f32[1,32,128]{2,1,0:T(8,128)}, bf16[16,128,128]{2,1,0:T(8,128)(2,1)}) custom-call(bf16[4,512,128]{2,1,0:T(8,128)(2,1)S(1)} %get-tuple-element.10.refs_0_, f32[7,128,128]{2,1,0:T(8,128)S(1)} %get-tuple-element.11.refs_1_, ...), custom_call_target="tpu_custom_call" | custom-call | tf_op jit(solution)/shard_map/hand_over/pallas_call | solution.py:426

commit v4 on v3

--- a/solution.py
+++ b/solution.py
@@ -13,8 +13,8 @@
 MESH = pl.DeviceIdType.MESH
 SWAP_AT = 4
 PASS_AT = 7
-TOPS_AT = 9
-FORWARD_AT = 16
+TOPS_AT = 15
+FORWARD_AT = 9
 EARLY = 1
 MAIN_VMEM = 54 << 20
 LAST_VMEM = 1 << 20

time: 41.8 us -> 41.4 us (level)
  no operation moved by 1% of the time
where the time goes in v4:
time: 41.4 us; the launch traced here: 41.3 us
  Pallas kernels  40.4 us (98%)
  between operations  0.8 us (2%)
    pallas_call x1, Pallas kernels, per_device(): pl.pallas_call(functools.partial(main_kernel, n_leaf), out_shape=[pltpu.V...  39.3 us
    pallas_call x1, Pallas kernels, per_device(): pl.pallas_call(last_kernel, out_shape=results, in_specs=[any_] * 5, out_s...  1.18 us

profile of v4, /device:TPU:2, one launch (start us, length us, event | category | flops | bytes accessed | tf_op | source)
XLA Modules:
  0.0 41.3 jit_solution(4891436247157603790)
XLA Ops:
  0.6 39.3 %factor_and_send.1 = (bf16[4,512,128]{2,1,0:T(8,128)(2,1)S(1)}, f32[7,128,128]{2,1,0:T(8,128)S(1)}, f32[2,32,128]{2,1,0:T(8,128)S(1)}, f32[1,32,128]{2,1,0:T(8,128)S(1)}, bf16[16,128,128]{2,1,0:T(8,128)(2,1)S(1)}) custom-call(s32[16]{0:T(128)} %row_ref.1, s32[16]{0:T(128)} %col_ref.1, bf16[4,512,128]{2,1,0:T(8,128)(2,1)} %leaf_hbm.1, ...), custom_call_target="tpu_custom_call" | custom-call | tf_op jit(solution)/shard_map/factor_and_send/pallas_call | solution.py:394
  39.9 1.2 %hand_over.1 = (bf16[4,512,128]{2,1,0:T(8,128)(2,1)}, f32[7,128,128]{2,1,0:T(8,128)}, f32[2,32,128]{2,1,0:T(8,128)}, f32[1,32,128]{2,1,0:T(8,128)}, bf16[16,128,128]{2,1,0:T(8,128)(2,1)}) custom-call(bf16[4,512,128]{2,1,0:T(8,128)(2,1)S(1)} %get-tuple-element.10.refs_0_, f32[7,128,128]{2,1,0:T(8,128)S(1)} %get-tuple-element.11.refs_1_, ...), custom_call_target="tpu_custom_call" | custom-call | tf_op jit(solution)/shard_map/hand_over/pallas_call | solution.py:426

commit v5 on v4

--- a/solution.py
+++ b/solution.py
@@ -304,10 +304,13 @@
 
     def project():
         load_own.wait()
-        for s in [*second, *direct]:
+        for s in second:
             s.wait_recv()
-        for i in range(16):
-            half_v[i] = halve(i)
+        for part in range(2):
+            for s in direct[2 * part : 2 * part + 2]:
+                s.wait_recv()
+            for i in [first + 4 * part + n for first in (0, 8) for n in range(4)]:
+                half_v[i] = halve(i)
         for h in halo[2:]:
             h.wait_recv()
         lane = lax.broadcasted_iota(jnp.int32, (16, N), 1)

time: 41.4 us -> 41.5 us (level)
  the two profiles are of different devices: /device:TPU:2 before, /device:TPU:24 now
where the time goes in v5:
time: 41.5 us; the launch traced here: 41.4 us
  Pallas kernels  40.6 us (98%)
  between operations  0.8 us (2%)
    pallas_call x1, Pallas kernels, per_device(): pl.pallas_call(functools.partial(main_kernel, n_leaf), out_shape=[pltpu.V...  39.4 us
    pallas_call x1, Pallas kernels, per_device(): pl.pallas_call(last_kernel, out_shape=results, in_specs=[any_] * 5, out_s...  1.18 us

profile of v5, /device:TPU:24, one launch (start us, length us, event | category | flops | bytes accessed | tf_op | source)
XLA Modules:
  0.0 41.4 jit_solution(10459642855572566961)
XLA Ops:
  0.6 39.4 %factor_and_send.1 = (bf16[4,512,128]{2,1,0:T(8,128)(2,1)S(1)}, f32[7,128,128]{2,1,0:T(8,128)S(1)}, f32[2,32,128]{2,1,0:T(8,128)S(1)}, f32[1,32,128]{2,1,0:T(8,128)S(1)}, bf16[16,128,128]{2,1,0:T(8,128)(2,1)S(1)}) custom-call(s32[16]{0:T(128)} %row_ref.1, s32[16]{0:T(128)} %col_ref.1, bf16[4,512,128]{2,1,0:T(8,128)(2,1)} %leaf_hbm.1, ...), custom_call_target="tpu_custom_call" | custom-call | tf_op jit(solution)/shard_map/factor_and_send/pallas_call | solution.py:397
  40.0 1.2 %hand_over.1 = (bf16[4,512,128]{2,1,0:T(8,128)(2,1)}, f32[7,128,128]{2,1,0:T(8,128)}, f32[2,32,128]{2,1,0:T(8,128)}, f32[1,32,128]{2,1,0:T(8,128)}, bf16[16,128,128]{2,1,0:T(8,128)(2,1)}) custom-call(bf16[4,512,128]{2,1,0:T(8,128)(2,1)S(1)} %get-tuple-element.10.refs_0_, f32[7,128,128]{2,1,0:T(8,128)S(1)} %get-tuple-element.11.refs_1_, ...), custom_call_target="tpu_custom_call" | custom-call | tf_op jit(solution)/shard_map/hand_over/pallas_call | solution.py:429
